TPU v7x, 32 devices: a whole 2x2x4 slice. The times are simulated.
32 devices in a mesh: frame: 2 (over core), patch: 8 (over z, x), tp: 2 (over y).
Axes of the slice: x: 2, y: 2, z: 4, core: 2. Of those that a mesh axis runs over, the one named last changes fastest.
Arguments:
- residual_codes: int32 [4, 16, 32, 1536], P('frame', 'patch', None, 'tp'), may hold values from -127 to 127
- exponents: int32 [4, 16, 32, 24], P('frame', 'patch', None, 'tp'), may hold values from -8 to -4
- conv_weight: bfloat16 [3, 3, 3, 1536], replicated, may hold values from -1.25 to 1.25
- timestep: int32 [4], P('frame'), may hold values from 0 to 49
- modulation: bfloat16 [50, 2, 1536], replicated, may hold values from -3 to 3
- query_weight: bfloat16 [1536, 768], P(None, 'tp')
- key_weight: bfloat16 [1536, 768], P(None, 'tp')
- value_weight: bfloat16 [1536, 768], P(None, 'tp'), may hold values from -0.15625 to 0.15625
Outputs:
- attended: bfloat16 [4, 16, 32, 768], P('frame', 'patch', None, 'tp')
All inputs are finite; a program needn't handle non-finite values.
Results may differ from a plain program's by a relative error of at most 0.02.
The roundings to bfloat16 on the way count: a program that leaves them out, or rounds other values in their place, can miss the bound.
Values may be sent and summed in bfloat16 or wider, within the bound.
A program may use at most 128 MiB of HBM per device.

v0:
```python
import jax
import jax.numpy as jnp
from jax import lax
from jax.sharding import PartitionSpec as P

HEAD_DIM = 64


def extended(x, sides, width):
    for axis, dim in sides:
        size, length = (lax.axis_size(axis), x.shape[dim])
        up = [(i, (i + 1) % size) for i in range(size - 1)]
        down = [(j, i) for i, j in up]
        last = lax.slice_in_dim(x, length - width, length, axis=dim)
        first = lax.slice_in_dim(x, 0, width, axis=dim)
        before = lax.ppermute(last, axis, up)
        after = lax.ppermute(first, axis, down)
        x = jnp.concatenate([before, x, after], axis=dim)
    return x


def dequantize(residual_codes, exponents):
    groups = exponents.shape[-1]
    channels = residual_codes.shape[-1]
    factor = jnp.exp2(exponents.astype(jnp.float32))
    values = residual_codes.astype(jnp.float32).reshape(
        residual_codes.shape[:-1] + (groups, channels // groups)
    )
    return (values * factor[..., None]).reshape(residual_codes.shape)


def convolve(padded, kernel, out_shape):
    frames, tile_rows, tile_cols = out_shape
    widened = jnp.pad(padded, ((0, 0), (0, 0), (1, 1), (0, 0)))
    result = jnp.zeros(out_shape + (kernel.shape[-1],), jnp.float32)
    for shift_f in range(3):
        for shift_h in range(3):
            for shift_w in range(3):
                window = widened[
                    shift_f : shift_f + frames,
                    shift_h : shift_h + tile_rows,
                    shift_w : shift_w + tile_cols,
                    :,
                ]
                result = result + window.astype(jnp.float32) * kernel[
                    shift_f, shift_h, shift_w
                ].astype(jnp.float32)
    return result


def modulate(mixed, modulation, timestep):
    selector = (
        jnp.arange(modulation.shape[0], dtype=jnp.int32)[None, :] == timestep[:, None]
    ).astype(jnp.float32)
    picked = jnp.einsum("fs,sjd->fjd", selector, modulation.astype(jnp.float32))
    shift_rows = picked[:, 0][:, None, None, :]
    scale_rows = picked[:, 1][:, None, None, :]
    values = mixed.astype(jnp.float32)
    average = jnp.mean(values, axis=-1, keepdims=True)
    centered = values - average
    variance = jnp.mean(centered * centered, axis=-1, keepdims=True)
    normed = centered / jnp.sqrt(variance + 1e-06) * (1.0 + scale_rows) + shift_rows
    return normed.astype(jnp.bfloat16)


def local(
    residual_codes,
    exponents,
    conv_weight,
    timestep,
    modulation,
    query_weight,
    key_weight,
    value_weight,
):
    frames, tile_rows, tile_cols, channels = residual_codes.shape
    model_width = conv_weight.shape[-1]
    local_width = query_weight.shape[1]
    local_heads = local_width // HEAD_DIM
    token_count = frames * tile_rows * tile_cols
    grid_shape = (frames, tile_rows, tile_cols)
    inputs_exact = dequantize(residual_codes, exponents)
    inputs_narrow = inputs_exact.astype(jnp.bfloat16)
    pair_index = lax.axis_index("tp")
    kernel = lax.dynamic_slice_in_dim(conv_weight, pair_index * channels, channels, 3)
    padded = extended(inputs_narrow, (("frame", 0), ("patch", 1)), 1)
    mixed_half = (inputs_exact + convolve(padded, kernel, grid_shape)).astype(jnp.bfloat16)
    mixed = lax.all_gather(mixed_half, "tp", axis=3, tiled=True)
    normed = modulate(mixed, modulation, timestep).reshape(token_count, model_width)
    queries = jnp.dot(normed, query_weight, preferred_element_type=jnp.float32).astype(jnp.bfloat16)
    key_local = jnp.dot(normed, key_weight, preferred_element_type=jnp.float32).astype(jnp.bfloat16)
    value_local = jnp.dot(normed, value_weight, preferred_element_type=jnp.float32).astype(
        jnp.bfloat16
    )
    score_scale = HEAD_DIM ** (-0.5)
    query_heads = queries.reshape(token_count, local_heads, HEAD_DIM)

    def fold_keys(state_tuple, shard_pair):
        running_max, running_sum, weighted = state_tuple
        key_part, value_part = shard_pair
        count_rows = key_part.shape[0]
        key_heads = key_part.reshape(count_rows, local_heads, HEAD_DIM)
        value_heads = value_part.reshape(count_rows, local_heads, HEAD_DIM)
        scores = (
            jnp.einsum("qhd,khd->hqk", query_heads, key_heads, preferred_element_type=jnp.float32)
            * score_scale
        )
        new_max = jnp.maximum(running_max, jnp.max(scores, axis=2))
        rescale = jnp.exp(running_max - new_max)
        exps = jnp.exp(scores - new_max[:, :, None])
        running_sum = running_sum * rescale + jnp.sum(exps, axis=2)
        update = jnp.einsum(
            "hqk,khd->qhd",
            exps.astype(jnp.bfloat16),
            value_heads,
            preferred_element_type=jnp.float32,
        )
        weighted = weighted * jnp.transpose(rescale)[:, :, None] + update
        return (new_max, running_sum, weighted)

    initial = (
        jnp.full((local_heads, token_count), -jnp.inf, jnp.float32),
        jnp.zeros((local_heads, token_count), jnp.float32),
        jnp.zeros((token_count, local_heads, HEAD_DIM), jnp.float32),
    )
    key_all, value_all = (
        lax.all_gather(key_local, "patch", axis=0, tiled=True),
        lax.all_gather(value_local, "patch", axis=0, tiled=True),
    )
    span_rows = 4 * token_count
    block_count = key_all.shape[0] // span_rows
    stacked = (
        key_all.reshape(block_count, span_rows, local_width),
        value_all.reshape(block_count, span_rows, local_width),
    )

    def visit(state_tuple, shard_pair):
        return (fold_keys(state_tuple, shard_pair), None)

    final_state, unused_out = lax.scan(visit, initial, stacked)
    weighted = final_state[2] / jnp.transpose(final_state[1])[:, :, None]
    return weighted.astype(jnp.bfloat16).reshape(frames, tile_rows, tile_cols, local_width)


def solution(mesh):
    in_specs = (
        P("frame", "patch", None, "tp"),
        P("frame", "patch", None, "tp"),
        P(),
        P("frame"),
        P(),
        P(None, "tp"),
        P(None, "tp"),
        P(None, "tp"),
    )
    out_specs = P("frame", "patch", None, "tp")
    return jax.shard_map(local, mesh=mesh, in_specs=in_specs, out_specs=out_specs, check_vma=False)
```

profile of v0, /device:TPU:0, one launch (start us, length us, event | category | flops | bytes accessed | tf_op | source)
XLA Modules:
  0.0 110.8 jit_solution(17362515741164255811)
XLA Ops:
  0.0 0.9 multiply_exponential_fusion
  0.9 0.1 copy.17
  1.0 0.3 mul.393
  1.3 0.0 copy-start.8
  1.4 0.3 mul.394
  1.7 2.4 %collective-permute-start = (bf16[1,2,32,768]{3,2,1,0:T(8,128)(2,1)S(1)}, bf16[1,2,32,768]{3,2,1,0:T(8,128)(2,1)S(1)}, u32[]{:S(2)}, u32[]{:S(2)}) collective-permute-start(bf16[1,2,32,768]{3,2,1,0:T(8,128)(2,1)S(1)} %get-tuple-element.134), channel_id=1, source_target_pairs={{0,16},{1,17},{2,18},{3,19},{4,20},{5,21},{6,22},{7,23},{8,24},{9,... | collective-permute-start | bytes 294920 | tf_op jit(solution)/shard_map/ppermute | solution.py:16
  4.1 1.3 %collective-permute-start.1 = (bf16[1,2,32,768]{3,2,1,0:T(8,128)(2,1)S(1)}, bf16[1,2,32,768]{3,2,1,0:T(8,128)(2,1)S(1)}, u32[]{:S(2)}, u32[]{:S(2)}) collective-permute-start(bf16[1,2,32,768]{3,2,1,0:T(8,128)(2,1)S(1)} %get-tuple-element.135), channel_id=1, source_target_pairs={{16,0},{17,1},{18,2},{19,3},{20,4},{21,5},{22,6},{23,7},{24,8},{25... | collective-permute-start | bytes 294920 | tf_op jit(solution)/shard_map/ppermute | solution.py:17
  5.4 0.2 fusion.20
  5.6 1.7 %collective-permute-done.1 = bf16[1,2,32,768]{3,2,1,0:T(8,128)(2,1)S(1)} collective-permute-done((bf16[1,2,32,768]{3,2,1,0:T(8,128)(2,1)S(1)}, bf16[1,2,32,768]{3,2,1,0:T(8,128)(2,1)S(1)}, u32[]{:S(2)}, u32[]{:S(2)}) %collective-permute-start.1) | collective-permute-done | bytes 98336 | tf_op jit(solution)/shard_map/ppermute | solution.py:17
  7.3 0.7 fusion.74
  8.0 4.2 %collective-permute-start.2 = (bf16[4,1,32,768]{3,2,1,0:T(8,128)(2,1)}, bf16[4,1,32,768]{3,2,1,0:T(8,128)(2,1)S(1)}, u32[]{:S(2)}, u32[]{:S(2)}) collective-permute-start(bf16[4,1,32,768]{3,2,1,0:T(8,128)(2,1)} %get-tuple-element.132), channel_id=1, source_target_pairs={{0,2},{2,4},{4,6},{6,8},{8,10},{10,12},{12,14},{1,3},{3,5},{5,7},{... | collective-permute-start | bytes 589832 | tf_op jit(solution)/shard_map/ppermute | solution.py:16
  12.3 1.3 %collective-permute-start.3 = (bf16[4,1,32,768]{3,2,1,0:T(8,128)(2,1)S(1)}, bf16[4,1,32,768]{3,2,1,0:T(8,128)(2,1)S(1)}, u32[]{:S(2)}, u32[]{:S(2)}) collective-permute-start(bf16[4,1,32,768]{3,2,1,0:T(8,128)(2,1)S(1)} %get-tuple-element.133), channel_id=1, source_target_pairs={{2,0},{4,2},{6,4},{8,6},{10,8},{12,10},{14,12},{3,1},{5,3},{7,5},{... | collective-permute-start | bytes 589832 | tf_op jit(solution)/shard_map/ppermute | solution.py:17
  13.6 0.3 fusion.27
  13.9 7.3 %collective-permute-done.2 = bf16[4,1,32,768]{3,2,1,0:T(8,128)(2,1)S(1)} collective-permute-done((bf16[4,1,32,768]{3,2,1,0:T(8,128)(2,1)}, bf16[4,1,32,768]{3,2,1,0:T(8,128)(2,1)S(1)}, u32[]{:S(2)}, u32[]{:S(2)}) %collective-permute-start.2) | collective-permute-done | bytes 196640 | tf_op jit(solution)/shard_map/ppermute | solution.py:16
  21.3 0.3 select_maximum_fusion.1
  21.6 0.1 maximum_maximum_fusion
  21.7 1.2 %add_convert_fusion = bf16[2,2,32,768]{3,2,1,0:T(8,128)(2,1)S(1)} fusion(bf16[2,2,32,768]{3,2,1,0:T(8,128)(2,1)S(1)} %fusion.22, bf16[4,4,34,768]{3,2,1,0:T(8,128)(2,1)S(1)} %select_maximum_fusion.1, bf16[4,3,32,768]{3,2,1,0:T(8,128)(2,1)S(1)} %get-tuple-element.131, bf16[1,2,32,768]{3,2,1,0:T(8,128)(2,1)S(1)} %collective-permute-done.1, ...), kind=kLoop, calls=%fused_computation.41 | loop fusion | flops 8454144 | bytes 6177792 | tf_op jit(solution)/shard_map/convert_element_type | solution.py:87
  22.9 6.3 %all_gather.9 = bf16[2,2,32,1536]{3,2,1,0:T(8,128)(2,1)S(1)} all-gather(bf16[2,2,32,768]{3,2,1,0:T(8,128)(2,1)S(1)} %add_convert_fusion), channel_id=1, replica_groups=mesh['frame'=2,'patch'=8,'tp'=2] {'tp'}, dimensions={3}, use_global_device_ids=true | all-gather | bytes 589824 | tf_op jit(solution)/shard_map/all_gather | solution.py:88
  29.2 0.1 convert_reduce_fusion
  29.4 0.3 fusion.16
  29.7 0.2 fusion.19
  29.9 0.0 copy-start.5
  29.9 0.4 convolution_convert_fusion
  30.3 0.2 copy-done.4
  30.5 0.4 convolution_convert_fusion.1
  30.9 0.4 copy-done.5
  31.3 0.4 convolution_convert_fusion.2
  31.7 0.8 copy.19
  32.4 35.5 %all_gather.10 = bf16[1024,384]{1,0:T(8,128)(2,1)S(1)} all-gather(bf16[128,384]{1,0:T(8,128)(2,1)S(1)} %convolution_convert_fusion.2), channel_id=1, replica_groups=mesh['frame'=2,'patch'=8,'tp'=2] {'patch'}, dimensions={0}, use_global_device_ids=true | all-gather | bytes 884736 | tf_op jit(solution)/shard_map/all_gather | solution.py:127
  67.9 31.9 %all_gather.11 = bf16[1024,384]{1,0:T(8,128)(2,1)S(1)} all-gather(bf16[128,384]{1,0:T(8,128)(2,1)S(1)} %convolution_convert_fusion), channel_id=1, replica_groups=mesh['frame'=2,'patch'=8,'tp'=2] {'patch'}, dimensions={0}, use_global_device_ids=true | all-gather | bytes 884736 | tf_op jit(solution)/shard_map/all_gather | solution.py:128
  99.9 9.0 %while.15 = (s32[]{:T(128)}, f32[6,128]{1,0:T(8,128)S(1)}, f32[6,128]{1,0:T(8,128)S(1)}, f32[128,6,64]{0,2,1:T(8,128)}, bf16[2,512,384]{2,1,0:T(8,128)(2,1)S(1)}...) while((s32[]{:T(128)}, f32[6,128]{1,0:T(8,128)S(1)}, ...), condition=%wide.region_5.6_spmd.clone, body=%wide.region_2.5_spmd.clone.sunk | while | flops 103174656 | bytes 15483053 | solution.py:140
  99.9 0.1 constant_dynamic-slice_fusion.22
  99.9 0.8 copy-done.1
  100.7 0.2 copy.30
  100.9 0.2 copy.31
  101.1 1.3 %bitcast_reduce_fusion.2 = (f32[6,128]{1,0:T(8,128)S(1)}, f32[6,512,128]{2,1,0:T(8,128)S(1)}) fusion(bf16[512,6,64]{0,2,1:T(8,128)(2,1)S(1)} %bitcast.60, bf16[128,6,64]{0,2,1:T(8,128)(2,1)} %get-tuple-element.216), kind=kOutput, calls=%fused_computation.1.clone.1 | convolution fusion | flops 51117312 | bytes 2067456 | tf_op jit(solution)/shard_map/while/body/eval_jaxpr/qhd,khd->hqk/dot_general | solution.py:105
  102.5 1.1 fusion.100
  103.6 0.2 fusion.98
  103.9 0.1 constant_dynamic-slice_fusion.22
  104.0 0.8 copy-done.1
  104.7 0.2 copy.30
  104.9 0.2 copy.31
  105.1 1.3 %bitcast_reduce_fusion.2 = (f32[6,128]{1,0:T(8,128)S(1)}, f32[6,512,128]{2,1,0:T(8,128)S(1)}) fusion(bf16[512,6,64]{0,2,1:T(8,128)(2,1)S(1)} %bitcast.60, bf16[128,6,64]{0,2,1:T(8,128)(2,1)} %get-tuple-element.216), kind=kOutput, calls=%fused_computation.1.clone.1 | convolution fusion | flops 51117312 | bytes 2067456 | tf_op jit(solution)/shard_map/while/body/eval_jaxpr/qhd,khd->hqk/dot_general | solution.py:105
  106.5 2.1 %fusion.100 = f32[128,6,64]{0,2,1:T(8,128)} fusion(bf16[512,6,64]{0,2,1:T(8,128)(2,1)S(1)} %bitcast.59, f32[6,512,128]{2,1,0:T(8,128)S(1)} %get-tuple-element.190, f32[6,128]{1,0:T(8,128)S(1)} %get-tuple-element.212, f32[128,6,64]{0,2,1:T(8,128)} %get-tuple-element.205, f32[128,6]{0,1:T(8,128)S(1)} %get-tuple-element.192, pred[]{:T(512)S(6)} %compare.56), kind=kOutput, calls=%fused_computation.7.clone.1 | convolution fusion | flops 51265536 | bytes 2365441 | tf_op jit(solution)/shard_map/while/body/eval_jaxpr/hqk,khd->qhd/dot_general | solution.py:112
  108.6 0.2 fusion.98
  108.8 1.0 divide_convert_fusion
  109.8 0.2 copy.22
  110.0 0.9 reshape.57
  (33 shorter events, 0.2 us)
Async XLA Ops:
  0.0 29.9 %copy-start = (bf16[1536,384]{1,0:T(8,128)(2,1)S(1)}, bf16[1536,384]{1,0:T(8,128)(2,1)}, u32[]{:S(2)}) copy-start(bf16[1536,384]{1,0:T(8,128)(2,1)} %param.17) | copy-start | bytes 3538948
  0.0 1.6 %copy-start.3 = (s32[2,2,32,768]{3,2,1,0:T(8,128)S(1)}, s32[2,2,32,768]{3,2,1,0:T(8,128)}, u32[]{:S(2)}) copy-start(s32[2,2,32,768]{3,2,1,0:T(8,128)} %param.10) | copy-start | bytes 1179652
  1.3 4.1 %copy-start.6 = (bf16[50,2,1536]{2,1,0:T(2,128)(2,1)S(1)}, bf16[50,2,1536]{2,1,0:T(2,128)(2,1)}, u32[]{:S(2)}) copy-start(bf16[50,2,1536]{2,1,0:T(2,128)(2,1)} %param.14) | copy-start | bytes 921604
  1.3 4.1 %copy-start.8 = (s32[2]{0:T(128)S(1)}, s32[2]{0:T(128)}, u32[]{:S(2)}) copy-start(s32[2]{0:T(128)} %param.13) | copy-start | bytes 28
  1.6 12.0 %copy-start.7 = (bf16[3,3,3,1536]{3,2,1,0:T(4,128)(2,1)S(1)}, bf16[3,3,3,1536]{3,2,1,0:T(4,128)(2,1)}, u32[]{:S(2)}) copy-start(bf16[3,3,3,1536]{3,2,1,0:T(4,128)(2,1)} %param.12) | copy-start | bytes 248836
  1.7 3.9 %collective-permute-start = (bf16[1,2,32,768]{3,2,1,0:T(8,128)(2,1)S(1)}, bf16[1,2,32,768]{3,2,1,0:T(8,128)(2,1)S(1)}, u32[]{:S(2)}, u32[]{:S(2)}) collective-permute-start(bf16[1,2,32,768]{3,2,1,0:T(8,128)(2,1)S(1)} %get-tuple-element.134), channel_id=1, source_target_pairs={{0,16},{1,17},{2,18},{3,19},{4,20},{5,21},{6,22},{7,23},{8,24},{9,... | collective-permute-start | bytes 294920 | tf_op jit(solution)/shard_map/ppermute | solution.py:16
  4.1 3.2 %collective-permute-start.1 = (bf16[1,2,32,768]{3,2,1,0:T(8,128)(2,1)S(1)}, bf16[1,2,32,768]{3,2,1,0:T(8,128)(2,1)S(1)}, u32[]{:S(2)}, u32[]{:S(2)}) collective-permute-start(bf16[1,2,32,768]{3,2,1,0:T(8,128)(2,1)S(1)} %get-tuple-element.135), channel_id=1, source_target_pairs={{16,0},{17,1},{18,2},{19,3},{20,4},{21,5},{22,6},{23,7},{24,8},{25... | collective-permute-start | bytes 294920 | tf_op jit(solution)/shard_map/ppermute | solution.py:17
  8.0 13.2 %collective-permute-start.2 = (bf16[4,1,32,768]{3,2,1,0:T(8,128)(2,1)}, bf16[4,1,32,768]{3,2,1,0:T(8,128)(2,1)S(1)}, u32[]{:S(2)}, u32[]{:S(2)}) collective-permute-start(bf16[4,1,32,768]{3,2,1,0:T(8,128)(2,1)} %get-tuple-element.132), channel_id=1, source_target_pairs={{0,2},{2,4},{4,6},{6,8},{8,10},{10,12},{12,14},{1,3},{3,5},{5,7},{... | collective-permute-start | bytes 589832 | tf_op jit(solution)/shard_map/ppermute | solution.py:16
  12.3 9.0 %collective-permute-start.3 = (bf16[4,1,32,768]{3,2,1,0:T(8,128)(2,1)S(1)}, bf16[4,1,32,768]{3,2,1,0:T(8,128)(2,1)S(1)}, u32[]{:S(2)}, u32[]{:S(2)}) collective-permute-start(bf16[4,1,32,768]{3,2,1,0:T(8,128)(2,1)S(1)} %get-tuple-element.133), channel_id=1, source_target_pairs={{2,0},{4,2},{6,4},{8,6},{10,8},{12,10},{14,12},{3,1},{5,3},{7,5},{... | collective-permute-start | bytes 589832 | tf_op jit(solution)/shard_map/ppermute | solution.py:17
  29.2 1.3 %copy-start.4 = (bf16[1536,384]{1,0:T(8,128)(2,1)S(1)}, bf16[1536,384]{1,0:T(8,128)(2,1)}, u32[]{:S(2)}) copy-start(bf16[1536,384]{1,0:T(8,128)(2,1)} %param.15) | copy-start | bytes 3538948
  29.9 1.4 %copy-start.5 = (bf16[1536,384]{1,0:T(8,128)(2,1)S(1)}, bf16[1536,384]{1,0:T(8,128)(2,1)}, u32[]{:S(2)}) copy-start(bf16[1536,384]{1,0:T(8,128)(2,1)} %param.16) | copy-start | bytes 3538948
  99.9 0.9 copy-start.1
  102.5 1.4 %copy-start.2 = (bf16[2,512,384]{2,1,0:T(8,128)(2,1)S(1)}, bf16[2,512,384]{2,1,0:T(8,128)(2,1)}, u32[]{:S(2)}) copy-start(bf16[2,512,384]{2,1,0:T(8,128)(2,1)} %copy-done.1) | copy-start | bytes 2359300 | tf_op jit(solution)/shard_map/while
  103.9 0.9 copy-start.1
  106.5 2.4 %copy-start.2 = (bf16[2,512,384]{2,1,0:T(8,128)(2,1)S(1)}, bf16[2,512,384]{2,1,0:T(8,128)(2,1)}, u32[]{:S(2)}) copy-start(bf16[2,512,384]{2,1,0:T(8,128)(2,1)} %copy-done.1) | copy-start | bytes 2359300 | tf_op jit(solution)/shard_map/while
where the time goes:
time: 111 us
  blocking collectives  73.8 us (66%)
  starting transfers between devices  9.17 us (8%)
  waiting for transfers between devices  9.01 us (8%)
  matrix products  7.18 us (6%)
  local copies, waits for them, and re-layouts  6.36 us (6%)
  other arithmetic  4.95 us (4%)
    all_gather x1, blocking collectives, local(): lax.all_gather(key_local, 'patch', axis=0, tiled=True)  35.5 us
    all_gather x1, blocking collectives, local(): lax.all_gather(value_local, 'patch', axis=0, tiled=True)  31.9 us
    ppermute x2, waiting for transfers between devices, extended(): before = lax.ppermute(last, axis, up)  7.35 us
    ppermute x2, starting transfers between devices, extended(): before = lax.ppermute(last, axis, up)  6.59 us
    all_gather x1, blocking collectives, local(): mixed = lax.all_gather(mixed_half, 'tp', axis=3, tiled=True)  6.35 us
    dot_general x2, matrix products, fold_keys(): jnp.einsum('hqk,khd->qhd', exps.astype(jnp.bfloat16), value_heads, prefer...  3.19 us
    dot_general x2, matrix products, fold_keys(): jnp.einsum('qhd,khd->hqk', query_heads, key_heads, preferred_element_type...  2.66 us
    ppermute x2, starting transfers between devices, extended(): after = lax.ppermute(first, axis, down)  2.58 us
  transfers between devices with their start and end apart: 4, of which 2 were waited for; matrix products, arithmetic and copies ran while one was open for 0% of the time, Pallas kernels for 0%

commit v1 on v0

v1 whole, which is shorter than its diff:
```python
import functools

import jax
import jax.numpy as jnp
from jax import lax
from jax.experimental import pallas as pl
from jax.experimental.pallas import tpu as pltpu
from jax.sharding import PartitionSpec as P

HEAD_DIM = 64
LANES = 128
MESH = pl.DeviceIdType.MESH


def flip(index, mask):
    bit = 1
    while bit <= mask:
        if mask & bit:
            index = index + bit - 2 * bit * lax.rem(lax.div(index, bit), 2)
        bit *= 2
    return index


def kernel(
    sizes,
    ts_hbm,
    codes_hbm,
    exps_hbm,
    taps_hbm,
    mod_hbm,
    wq_hbm,
    wk_hbm,
    wv_hbm,
    out_ref,
    ts_ref,
    codes_ref,
    exps_ref,
    taps_ref,
    mod_ref,
    pad,
    taps,
    mixed,
    normed,
    wkv,
    wq,
    kv_own,
    kv_all,
    q_own,
    q_pack,
    q_peer,
    o_pack,
    o_peer,
    in_sem,
    row_send,
    row_recv,
    frame_send,
    frame_recv,
    corner_send,
    corner_recv,
    mix_send,
    mix_recv,
    a_send,
    a_recv,
    b_send,
    b_recv,
    c_send,
    c_recv,
    q_send,
    q_recv,
    o_send,
    o_recv,
):
    n_frame, n_patch, n_tp = sizes
    frames, rows, cols, channels = codes_ref.shape
    tokens = frames * rows * cols
    half = rows * cols
    local_width = wq_hbm.shape[1]
    local_heads = local_width // HEAD_DIM
    heads = local_heads // 2
    width = n_tp * channels
    f_me = lax.axis_index("frame")
    p_me = lax.axis_index("patch")
    t_me = lax.axis_index("tp")
    t_peer = 1 - t_me
    side = lax.rem(lax.div(p_me, 2), 2)
    lead = lax.rem(f_me, 2)
    order = (lead, 1 - lead)
    p_pair = flip(p_me, 2)
    p_twin = flip(p_me, 1)
    far = list(range(4, n_patch, 4))

    loads = [
        pltpu.make_async_copy(src, dst, in_sem.at[i])
        for i, (src, dst) in enumerate(
            [
                (codes_hbm, codes_ref),
                (exps_hbm, exps_ref),
                (taps_hbm, taps_ref),
                (ts_hbm, ts_ref),
                (mod_hbm, mod_ref),
                (wk_hbm, wkv.at[:, pl.ds(0, local_width)]),
                (wv_hbm, wkv.at[:, pl.ds(local_width, local_width)]),
                (wq_hbm, wq),
            ]
        )
    ]
    for copy in loads:
        copy.start()

    barrier = pltpu.get_barrier_semaphore()

    def signal(f, p, t):
        pl.semaphore_signal(barrier, inc=1, device_id=(f, p, t), device_id_type=MESH)

    f_there = {-1: f_me > 0, 1: f_me < n_frame - 1}
    p_there = {-1: p_me > 0, 1: p_me < n_patch - 1}
    count = 3 + 2 * len(far)
    for d in (-1, 1):

        @pl.when(f_there[d])
        def _():
            signal(f_me + d, p_me, t_me)

        @pl.when(p_there[d])
        def _():
            signal(f_me, p_me + d, t_me)

        count = count + f_there[d].astype(jnp.int32) + p_there[d].astype(jnp.int32)
    signal(f_me, p_me, t_peer)
    signal(f_me, p_pair, t_me)
    signal(f_me, p_twin, t_me)
    for k in far:
        signal(f_me, flip(p_me, k), t_me)
        signal(f_me, flip(p_me, k + 2), t_me)

    for d in (-1, 1):
        edge_f = 0 if d < 0 else frames + 1
        edge_r = 0 if d < 0 else rows + 1

        @pl.when(jnp.logical_not(f_there[d]))
        def _():
            pad[edge_f] = jnp.zeros((rows + 2, cols, channels), jnp.bfloat16)

        @pl.when(jnp.logical_not(p_there[d]))
        def _():
            pad[1 : 1 + frames, edge_r] = jnp.zeros((frames, cols, channels), jnp.bfloat16)
            for g in (-1, 1):

                @pl.when(f_there[g])
                def _():
                    pad[0 if g < 0 else frames + 1, edge_r] = jnp.zeros(
                        (cols, channels), jnp.bfloat16
                    )

    groups = exps_ref.shape[1]
    span = channels // groups
    spread = (
        lax.broadcasted_iota(jnp.int32, (groups, channels), 1) // span
        == lax.broadcasted_iota(jnp.int32, (groups, channels), 0)
    ).astype(jnp.float32).astype(jnp.bfloat16)
    loads[0].wait()
    loads[1].wait()
    for f in range(frames):
        for r in range(rows):
            factor = jnp.left_shift(jnp.ones((groups, cols), jnp.int32), exps_ref[f, :, r, :] + 8)
            factor = (factor.astype(jnp.float32) * (2.0**-8)).astype(jnp.bfloat16)
            factor = lax.dot_general(
                factor, spread, (((0,), (0,)), ((), ())), preferred_element_type=jnp.float32
            )
            values = codes_ref[f, r].astype(jnp.float32) * factor
            pad[f + 1, r + 1] = values.astype(jnp.bfloat16)

    pl.semaphore_wait(barrier, count)

    def row_copy(d, part):
        frame = 1 + order[1 - part]
        number = (0 if d < 0 else 2) + part
        return pltpu.make_async_remote_copy(
            src_ref=pad.at[frame, rows if d > 0 else 1],
            dst_ref=pad.at[frame, 0 if d > 0 else rows + 1],
            send_sem=row_send.at[number],
            recv_sem=row_recv.at[number],
            device_id=(f_me, p_me + d, t_me),
            device_id_type=MESH,
        )

    def frame_copy(d):
        number = 0 if d < 0 else 1
        return pltpu.make_async_remote_copy(
            src_ref=pad.at[frames if d > 0 else 1, pl.ds(1, rows)],
            dst_ref=pad.at[0 if d > 0 else frames + 1, pl.ds(1, rows)],
            send_sem=frame_send.at[number],
            recv_sem=frame_recv.at[number],
            device_id=(f_me + d, p_me, t_me),
            device_id_type=MESH,
        )

    def corner_copy(d, g):
        number = (0 if d < 0 else 2) + (0 if g < 0 else 1)
        row = 0 if g > 0 else rows + 1
        return pltpu.make_async_remote_copy(
            src_ref=pad.at[frames if d > 0 else 1, row],
            dst_ref=pad.at[0 if d > 0 else frames + 1, row],
            send_sem=corner_send.at[number],
            recv_sem=corner_recv.at[number],
            device_id=(f_me + d, p_me, t_me),
            device_id_type=MESH,
        )

    for part in range(2):
        for d in (-1, 1):
            pl.when(p_there[d])(row_copy(d, part).start)
    for d in (-1, 1):
        pl.when(f_there[d])(frame_copy(d).start)

    loads[2].wait()
    own_lanes = pl.ds(pl.multiple_of(t_me * channels, LANES), channels)
    for a in range(3):
        for b in range(3):
            taps[a * 3 + b] = taps_ref[a, b, :, own_lanes].astype(jnp.float32)

    for part in range(2):
        for g in (-1, 1):
            pl.when(p_there[-g])(row_copy(g, part).wait_recv)
            for d in (-1, 1):
                first = (lead == 1) if d < 0 else (lead == 0)
                mine = first if part == 0 else jnp.logical_not(first)
                ready = jnp.logical_and(jnp.logical_and(p_there[-g], f_there[d]), mine)
                pl.when(ready)(corner_copy(d, g).start)
    for d in (-1, 1):
        pl.when(f_there[-d])(frame_copy(d).wait_recv)

    col = lax.broadcasted_iota(jnp.int32, (cols, LANES), 0)

    def mix_copy(part, r, t):
        i = order[part] * rows + r
        return pltpu.make_async_remote_copy(
            src_ref=mixed.at[i, t],
            dst_ref=mixed.at[i, t],
            send_sem=mix_send.at[part * rows + r],
            recv_sem=mix_recv.at[part * rows + r],
            device_id=(f_me, p_me, t_peer),
            device_id_type=MESH,
        )

    for part in range(2):
        f = order[part]
        for d in (-1, 1):
            for g in (-1, 1):
                needs = (f == 0) if d > 0 else (f == frames - 1)
                ready = jnp.logical_and(jnp.logical_and(p_there[-g], f_there[-d]), needs)
                pl.when(ready)(corner_copy(d, g).wait_recv)
        for r in range(rows):

            def conv(step, carry):
                at = pl.ds(pl.multiple_of(step * LANES, LANES), LANES)
                sums = [jnp.zeros((cols, LANES), jnp.float32) for _ in range(3)]
                centre = None
                for a in range(3):
                    for b in range(3):
                        x = pad[f + a, r + b, :, at].astype(jnp.float32)
                        if a == 1 and b == 1:
                            centre = x
                        w = taps[a * 3 + b, :, at]
                        for c in range(3):
                            sums[c] = sums[c] + x * w[c : c + 1]
                before = jnp.where(col == 0, 0.0, pltpu.roll(sums[0], 1, 0))
                after = jnp.where(col == cols - 1, 0.0, pltpu.roll(sums[2], cols - 1, 0))
                total = centre + (sums[1] + (before + after))
                mixed[f * rows + r, t_me, :, at] = total.astype(jnp.bfloat16)
                return carry

            lax.fori_loop(0, channels // LANES, conv, 0)
            mix_copy(part, r, t_me).start()

    started = []

    def go(src, dst, s_sem, r_sem, p):
        copy = pltpu.make_async_remote_copy(
            src_ref=src,
            dst_ref=dst,
            send_sem=s_sem,
            recv_sem=r_sem,
            device_id=(f_me, p, t_me),
            device_id_type=MESH,
        )
        copy.start()
        started.append(copy)
        return copy

    pieces = [(0, pl.ds(0, heads))] + [(1, pl.ds(h, 1)) for h in range(heads)]
    arrivals = {}

    def beside(n, slot):
        part, hs = pieces[n]
        at = pl.ds(part * half, half)
        arrivals[n, slot + 1] = go(
            kv_all.at[hs, slot, at],
            kv_all.at[hs, slot + 1, at],
            c_send.at[n, slot // 2],
            c_recv.at[n, slot // 2],
            p_twin,
        )

    def spread_piece(n):
        part, hs = pieces[n]
        at = pl.ds(part * half, half)
        size = heads if part == 0 else 1
        first = 0 if part == 0 else n - 1
        mine = pl.ds(side * heads + first, size)
        other = pl.ds((1 - side) * heads + first, size)
        for m, k in enumerate(far):
            for slot, src in ((0, mine), (2, other)):
                arrivals[n, k + slot] = go(
                    kv_own.at[src, at],
                    kv_all.at[hs, k + slot, at],
                    b_send.at[n, 2 * m + slot // 2],
                    b_recv.at[n, 2 * m + slot // 2],
                    flip(p_me, k + slot),
                )
        arrivals[n, 2] = go(
            kv_own.at[other, at], kv_all.at[hs, 2, at], a_send.at[n], a_recv.at[n], p_pair
        )
        beside(n, 0)

    for part in range(2):
        f = order[part]
        if part == 0:
            loads[3].wait()
            loads[4].wait()
        picked = mod_ref[ts_ref[f]].astype(jnp.float32)
        shift, scale = picked[0:1], 1.0 + picked[1:2]
        for r in range(rows):
            mix_copy(part, r, t_peer).wait_recv()
            xs = [mixed[f * rows + r, t].astype(jnp.float32) for t in range(n_tp)]
            mean = sum(jnp.sum(x, axis=1, keepdims=True) for x in xs) * (1.0 / width)
            xs = [x - mean for x in xs]
            var = sum(jnp.sum(x * x, axis=1, keepdims=True) for x in xs) * (1.0 / width)
            inv = 1.0 / jnp.sqrt(var + 1e-06)
            for t in range(n_tp):
                at = slice(t * channels, (t + 1) * channels)
                y = xs[t] * inv * scale[:, at] + shift[:, at]
                row = part * half + r * cols
                normed[row : row + cols, at] = y.astype(jnp.bfloat16)
        if part == 0:
            loads[5].wait()
            loads[6].wait()
        at = slice(part * half, (part + 1) * half)
        kv = jnp.dot(normed[at], wkv[...], preferred_element_type=jnp.float32)
        for h in range(local_heads):
            k_at = h * HEAD_DIM
            v_at = local_width + h * HEAD_DIM
            kv_own[h, at] = jnp.concatenate(
                [kv[:, k_at : k_at + HEAD_DIM], kv[:, v_at : v_at + HEAD_DIM]], axis=1
            ).astype(jnp.bfloat16)
        for h in range(heads):
            kv_all[h, 0, at] = kv_own[side * heads + h, at]
        for n, (piece_part, _) in enumerate(pieces):
            if piece_part == part:
                spread_piece(n)

    def relay(n):
        for slot in [2] + [k + s for k in far for s in (0, 2)]:
            arrivals[n, slot].wait_recv()
            beside(n, slot)

    relay(0)

    loads[7].wait()
    q = jnp.dot(normed[...], wq[...], preferred_element_type=jnp.float32)
    q = q.astype(jnp.bfloat16).astype(jnp.float32) * (HEAD_DIM**-0.5)
    blank = jnp.zeros((tokens, HEAD_DIM), jnp.float32)
    for h in range(local_heads):
        q_h = q[:, h * HEAD_DIM : (h + 1) * HEAD_DIM]
        q_own[h] = jnp.concatenate([q_h, blank], axis=1).astype(jnp.bfloat16)
        q_pack[h] = jnp.concatenate([q_h[:half], q_h[half:]], axis=1).astype(jnp.bfloat16)
    q_copy = go(
        q_pack.at[pl.ds((1 - side) * heads, heads)], q_peer, q_send.at[0], q_recv.at[0], p_pair
    )

    for n in range(1, len(pieces)):
        relay(n)

    q_copy.wait_recv()
    for slot in range(1, n_patch, 2):
        arrivals[0, slot].wait_recv()
    o_copies = []
    own = []
    zeros = jnp.zeros((half, HEAD_DIM), jnp.float32)
    for h in range(heads):
        for slot in range(1, n_patch, 2):
            arrivals[h + 1, slot].wait_recv()
        packed = q_peer[h].astype(jnp.float32)
        peer = jnp.concatenate(
            [
                jnp.concatenate([packed[:, :HEAD_DIM], zeros], axis=1),
                jnp.concatenate([packed[:, HEAD_DIM:], zeros], axis=1),
            ],
            axis=0,
        ).astype(jnp.bfloat16)
        queries = jnp.concatenate([peer, q_own[side * heads + h]], axis=0)
        rows_kv = kv_all[h].reshape(n_patch * tokens, 2 * HEAD_DIM)
        scores = lax.dot_general(
            queries, rows_kv, (((1,), (1,)), ((), ())), preferred_element_type=jnp.float32
        )
        exps = jnp.exp(scores - jnp.max(scores, axis=1, keepdims=True))
        totals = jnp.sum(exps, axis=1, keepdims=True)
        summed = jnp.dot(
            exps.astype(jnp.bfloat16), rows_kv, preferred_element_type=jnp.float32
        )
        result = summed[:, HEAD_DIM:] / totals
        o_pack[h] = jnp.concatenate(
            [result[:half], result[half:tokens]], axis=1
        ).astype(jnp.bfloat16)
        o_copies.append(go(o_pack.at[h], o_peer.at[h], o_send.at[h], o_recv.at[h], p_pair))
        own.append(result[tokens:])

    for d in (-1, 1):
        for part in range(2):
            pl.when(p_there[d])(row_copy(d, part).wait_send)
        pl.when(f_there[d])(frame_copy(d).wait_send)
        for g in (-1, 1):
            pl.when(jnp.logical_and(p_there[-g], f_there[d]))(corner_copy(d, g).wait_send)
    for part in range(2):
        for r in range(rows):
            mix_copy(part, r, t_me).wait_send()
    for copy in started:
        copy.wait_send()

    others = []
    for h in range(heads):
        o_copies[h].wait_recv()
        packed = o_peer[h].astype(jnp.float32)
        others.append(jnp.concatenate([packed[:, :HEAD_DIM], packed[:, HEAD_DIM:]], axis=0))
    low = jnp.concatenate(own + others, axis=1)
    high = jnp.concatenate(others + own, axis=1)
    final = jnp.where(side == 0, low, high).astype(jnp.bfloat16)
    for part in range(2):
        piece = final[part * half : (part + 1) * half]
        out_ref[order[part]] = piece.reshape(rows, cols, local_width)


def solution(mesh):
    sizes = tuple(mesh.shape[a] for a in ("frame", "patch", "tp"))
    n_patch = sizes[1]
    far = max(1, n_patch // 4 - 1)

    def local(codes, exps, taps, timestep, modulation, wq, wk, wv):
        frames, rows, cols, channels = codes.shape
        tokens = frames * rows * cols
        width, local_width = wq.shape
        local_heads = local_width // HEAD_DIM
        heads = local_heads // 2
        exps = jnp.transpose(exps, (0, 3, 1, 2))
        bf, f32 = jnp.bfloat16, jnp.float32
        hbm = pl.BlockSpec(memory_space=pltpu.HBM)
        dma = pltpu.SemaphoreType.DMA
        macs = tokens * width * local_width * 3
        macs += 2 * tokens * tokens * n_patch * local_heads * 2 * HEAD_DIM
        return pl.pallas_call(
            functools.partial(kernel, sizes),
            out_shape=jax.ShapeDtypeStruct((frames, rows, cols, local_width), bf),
            in_specs=[hbm] * 8,
            out_specs=pl.BlockSpec(memory_space=pltpu.VMEM),
            scratch_shapes=[
                pltpu.SMEM(timestep.shape, jnp.int32),
                pltpu.VMEM(codes.shape, jnp.int32),
                pltpu.VMEM(exps.shape, jnp.int32),
                pltpu.VMEM(taps.shape, bf),
                pltpu.VMEM(modulation.shape, bf),
                pltpu.VMEM((frames + 2, rows + 2, cols, channels), bf),
                pltpu.VMEM((9, 3, channels), f32),
                pltpu.VMEM((frames * rows, sizes[2], cols, channels), bf),
                pltpu.VMEM((tokens, width), bf),
                pltpu.VMEM((width, 2 * local_width), bf),
                pltpu.VMEM((width, local_width), bf),
                pltpu.VMEM((local_heads, tokens, LANES), bf),
                pltpu.VMEM((heads, n_patch, tokens, LANES), bf),
                pltpu.VMEM((local_heads, tokens, LANES), bf),
                pltpu.VMEM((local_heads, tokens // 2, LANES), bf),
                pltpu.VMEM((heads, tokens // 2, LANES), bf),
                pltpu.VMEM((heads, tokens // 2, LANES), bf),
                pltpu.VMEM((heads, tokens // 2, LANES), bf),
                dma((8,)),
                dma((4,)),
                dma((4,)),
                dma((2,)),
                dma((2,)),
                dma((4,)),
                dma((4,)),
                dma((frames * rows,)),
                dma((frames * rows,)),
                dma((heads + 1,)),
                dma((heads + 1,)),
                dma((heads + 1, 2 * far)),
                dma((heads + 1, 2 * far)),
                dma((heads + 1, n_patch // 2)),
                dma((heads + 1, n_patch // 2)),
                dma((1,)),
                dma((1,)),
                dma((heads,)),
                dma((heads,)),
            ],
            compiler_params=pltpu.CompilerParams(
                collective_id=0, has_side_effects=True, vmem_limit_bytes=56 * 1024 * 1024
            ),
            cost_estimate=pl.CostEstimate(
                flops=2 * macs, bytes_accessed=width * local_width * 6, transcendentals=0
            ),
        )(timestep, codes, exps, taps, modulation, wq, wk, wv)

    in_specs = (
        P("frame", "patch", None, "tp"),
        P("frame", "patch", None, "tp"),
        P(),
        P("frame"),
        P(),
        P(None, "tp"),
        P(None, "tp"),
        P(None, "tp"),
    )
    out_specs = P("frame", "patch", None, "tp")
    return jax.shard_map(local, mesh=mesh, in_specs=in_specs, out_specs=out_specs, check_vma=False)
```

time: 111 us -> 35.6 us (0.32)
  blocking collectives: 73.8 us -> 0 us
  Pallas kernels: 0 us -> 33.9 us
  starting transfers between devices: 9.17 us -> 0 us
  waiting for transfers between devices: 9.01 us -> 0 us
  matrix products: 7.18 us -> 0 us
  other arithmetic: 4.95 us -> 0 us
  local copies, waits for them, and re-layouts: 6.36 us -> 1.54 us
    all_gather x3 -> x0, blocking collectives: 73.8 us -> none  [the longest x1 35.5 us: local(): lax.all_gather(key_local, 'patch', axis=0, tiled=True)]
    pallas_call x0 -> x1, Pallas kernels: none -> 33.9 us  [local(): pl.pallas_call(functools.partial(kernel, sizes), out_shape=jax.ShapeDtype...]
    ppermute x4 -> x0, starting transfers between devices: 9.17 us -> none  [the longest x2 6.59 us: extended(): before = lax.ppermute(last, axis, up)]
    ppermute x4 -> x0, waiting for transfers between devices: 9.01 us -> none  [the longest x2 7.35 us: extended(): before = lax.ppermute(last, axis, up)]
    dot_general x8 -> x0, matrix products: 7.18 us -> none  [the longest x2 3.19 us: fold_keys(): jnp.einsum('hqk,khd->qhd', exps.astype(jnp.bfloat16), value_heads, prefer...]
    convert_element_type x4 -> x0, other arithmetic: 2.4 us -> none  [the longest x1 1.16 us: local(): (inputs_exact + convolve(padded, kernel, grid_shape)).astype(jnp.bfloat16)]
    while x10 -> x0, local copies, waits for them, and re-layouts: 1.57 us -> none
  transfers between devices with their start and end apart: 4 -> 0, of which waited for: 2 -> 0; matrix products, arithmetic and copies ran while one was open for 0% -> 0% of each run, Pallas kernels for 0% -> 0%
where the time goes in v1:
time: 35.6 us; the launch traced here: 35.5 us
  Pallas kernels  33.9 us (95%)
  local copies, waits for them, and re-layouts  1.54 us (4%)
    pallas_call x1, Pallas kernels, local(): pl.pallas_call(functools.partial(kernel, sizes), out_shape=jax.ShapeDtype...  33.9 us
    unnamed x1, local copies, waits for them, and re-layouts  1.54 us

profile of v1, /device:TPU:0, one launch (start us, length us, event | category | flops | bytes accessed | tf_op | source)
XLA Modules:
  0.0 35.5 jit_solution(16579593558429903426)
XLA Ops:
  0.0 33.9 %shard_map.82 = bf16[2,2,32,384]{3,2,1,0:T(8,128)(2,1)} custom-call(s32[2]{0:T(128)} %ts_hbm.1, s32[2,2,32,768]{3,2,1,0:T(8,128)} %codes_hbm.1, s32[2,12,2,32]{3,2,1,0:T(2,128)} %bitcast.1, bf16[3,3,3,1536]{3,2,1,0:T(4,128)(2,1)} %taps_hbm.1, bf16[50,2,1536]{2,1,0:T(2,128)(2,1)} %mod_hbm.1, bf16[1536,384]{1,0:T(8,128)(2,1)} %wq_hbm.1, ...), custom_call_target="tpu_custom_call" | custom-call | flops 855638016 | bytes 3538944 | tf_op jit(solution)/shard_map/pallas_call | solution.py:460
  33.9 1.5 %copy.10 = bf16[2,2,32,384]{3,2,1,0:T(8,128)(2,1)} copy(bf16[2,2,32,384]{3,2,1,0:T(8,128)(2,1)} %shard_map.82) | data formatting | bytes 196608

commit v2 on v1

--- a/solution.py
+++ b/solution.py
@@ -73,7 +73,7 @@
     n_frame, n_patch, n_tp = sizes
     frames, rows, cols, channels = codes_ref.shape
     tokens = frames * rows * cols
-    half = rows * cols
+    half = tokens // 2
     local_width = wq_hbm.shape[1]
     local_heads = local_width // HEAD_DIM
     heads = local_heads // 2
@@ -83,8 +83,12 @@
     t_me = lax.axis_index("tp")
     t_peer = 1 - t_me
     side = lax.rem(lax.div(p_me, 2), 2)
-    lead = lax.rem(f_me, 2)
-    order = (lead, 1 - lead)
+    p_odd = lax.rem(p_me, 2)
+    f_odd = lax.rem(f_me, 2)
+    order = (1 - p_odd, p_odd)
+    edge = ((rows + 1) * (1 - p_odd), (rows + 1) * p_odd)
+    p_next = p_me - 1 + 2 * p_odd
+    next_there = jnp.logical_and(p_next >= 0, p_next < n_patch)
     p_pair = flip(p_me, 2)
     p_twin = flip(p_me, 1)
     far = list(range(4, n_patch, 4))
@@ -93,7 +97,7 @@
         pltpu.make_async_copy(src, dst, in_sem.at[i])
         for i, (src, dst) in enumerate(
             [
-                (codes_hbm, codes_ref),
+                (codes_hbm.at[:, order[0]], codes_ref.at[:, order[0]]),
                 (exps_hbm, exps_ref),
                 (taps_hbm, taps_ref),
                 (ts_hbm, ts_ref),
@@ -101,11 +105,12 @@
                 (wk_hbm, wkv.at[:, pl.ds(0, local_width)]),
                 (wv_hbm, wkv.at[:, pl.ds(local_width, local_width)]),
                 (wq_hbm, wq),
+                (codes_hbm.at[:, order[1]], codes_ref.at[:, order[1]]),
             ]
         )
     ]
-    for copy in loads:
-        copy.start()
+    for i in (0, 1, 8, 2, 3, 4, 5, 6, 7):
+        loads[i].start()
 
     barrier = pltpu.get_barrier_semaphore()
 
@@ -113,19 +118,19 @@
         pl.semaphore_signal(barrier, inc=1, device_id=(f, p, t), device_id_type=MESH)
 
     f_there = {-1: f_me > 0, 1: f_me < n_frame - 1}
-    p_there = {-1: p_me > 0, 1: p_me < n_patch - 1}
-    count = 3 + 2 * len(far)
+    count = 3 + 2 * len(far) + next_there.astype(jnp.int32)
     for d in (-1, 1):
 
         @pl.when(f_there[d])
         def _():
             signal(f_me + d, p_me, t_me)
 
-        @pl.when(p_there[d])
-        def _():
-            signal(f_me, p_me + d, t_me)
-
-        count = count + f_there[d].astype(jnp.int32) + p_there[d].astype(jnp.int32)
+        count = count + f_there[d].astype(jnp.int32)
+
+    @pl.when(next_there)
+    def _():
+        signal(f_me, p_next, t_me)
+
     signal(f_me, p_me, t_peer)
     signal(f_me, p_pair, t_me)
     signal(f_me, p_twin, t_me)
@@ -134,23 +139,15 @@
         signal(f_me, flip(p_me, k + 2), t_me)
 
     for d in (-1, 1):
-        edge_f = 0 if d < 0 else frames + 1
-        edge_r = 0 if d < 0 else rows + 1
 
         @pl.when(jnp.logical_not(f_there[d]))
         def _():
-            pad[edge_f] = jnp.zeros((rows + 2, cols, channels), jnp.bfloat16)
-
-        @pl.when(jnp.logical_not(p_there[d]))
-        def _():
-            pad[1 : 1 + frames, edge_r] = jnp.zeros((frames, cols, channels), jnp.bfloat16)
-            for g in (-1, 1):
-
-                @pl.when(f_there[g])
-                def _():
-                    pad[0 if g < 0 else frames + 1, edge_r] = jnp.zeros(
-                        (cols, channels), jnp.bfloat16
-                    )
+            pad[0 if d < 0 else frames + 1] = jnp.zeros((rows + 2, cols, channels), jnp.bfloat16)
+
+    @pl.when(jnp.logical_not(next_there))
+    def _():
+        for f in range(frames + 2):
+            pad[f, edge[1]] = jnp.zeros((cols, channels), jnp.bfloat16)
 
     groups = exps_ref.shape[1]
     span = channels // groups
@@ -158,11 +155,14 @@
         lax.broadcasted_iota(jnp.int32, (groups, channels), 1) // span
         == lax.broadcasted_iota(jnp.int32, (groups, channels), 0)
     ).astype(jnp.float32).astype(jnp.bfloat16)
-    loads[0].wait()
     loads[1].wait()
-    for f in range(frames):
-        for r in range(rows):
-            factor = jnp.left_shift(jnp.ones((groups, cols), jnp.int32), exps_ref[f, :, r, :] + 8)
+
+    def dequantize(part):
+        r = order[part]
+        loads[0 if part == 0 else 8].wait()
+        for f in range(frames):
+            power = jnp.where(r == 0, exps_ref[f, :, 0, :], exps_ref[f, :, 1, :])
+            factor = jnp.left_shift(jnp.ones((groups, cols), jnp.int32), power + 8)
             factor = (factor.astype(jnp.float32) * (2.0**-8)).astype(jnp.bfloat16)
             factor = lax.dot_general(
                 factor, spread, (((0,), (0,)), ((), ())), preferred_element_type=jnp.float32
@@ -170,48 +170,71 @@
             values = codes_ref[f, r].astype(jnp.float32) * factor
             pad[f + 1, r + 1] = values.astype(jnp.bfloat16)
 
-    pl.semaphore_wait(barrier, count)
-
-    def row_copy(d, part):
-        frame = 1 + order[1 - part]
-        number = (0 if d < 0 else 2) + part
+    def remote(src, dst, s_sem, r_sem, device):
         return pltpu.make_async_remote_copy(
-            src_ref=pad.at[frame, rows if d > 0 else 1],
-            dst_ref=pad.at[frame, 0 if d > 0 else rows + 1],
-            send_sem=row_send.at[number],
-            recv_sem=row_recv.at[number],
-            device_id=(f_me, p_me + d, t_me),
+            src_ref=src,
+            dst_ref=dst,
+            send_sem=s_sem,
+            recv_sem=r_sem,
+            device_id=device,
             device_id_type=MESH,
         )
 
-    def frame_copy(d):
-        number = 0 if d < 0 else 1
-        return pltpu.make_async_remote_copy(
-            src_ref=pad.at[frames if d > 0 else 1, pl.ds(1, rows)],
-            dst_ref=pad.at[0 if d > 0 else frames + 1, pl.ds(1, rows)],
-            send_sem=frame_send.at[number],
-            recv_sem=frame_recv.at[number],
-            device_id=(f_me + d, p_me, t_me),
-            device_id_type=MESH,
-        )
-
-    def corner_copy(d, g):
-        number = (0 if d < 0 else 2) + (0 if g < 0 else 1)
-        row = 0 if g > 0 else rows + 1
-        return pltpu.make_async_remote_copy(
-            src_ref=pad.at[frames if d > 0 else 1, row],
-            dst_ref=pad.at[0 if d > 0 else frames + 1, row],
-            send_sem=corner_send.at[number],
-            recv_sem=corner_recv.at[number],
-            device_id=(f_me + d, p_me, t_me),
-            device_id_type=MESH,
-        )
+    frame_of = (2 - f_odd, 1 + f_odd)
+
+    def row_copy(part, m, arriving):
+        row = edge[part] if arriving else order[part] + 1
+        return remote(
+            pad.at[frame_of[m], row],
+            pad.at[frame_of[m], edge[part] if arriving else rows + 1 - edge[part]],
+            row_send.at[2 * part + m],
+            row_recv.at[2 * part + m],
+            (f_me, p_twin if part == 0 else p_next, t_me),
+        )
+
+    f_target = (f_me + 1 - 2 * f_odd, f_me - 1 + 2 * f_odd)
+    f_ok = tuple(jnp.logical_and(f >= 0, f < n_frame) for f in f_target)
+    f_edge = ((frames + 1) * (1 - f_odd), (frames + 1) * f_odd)
+
+    def frame_copy(part, m, row, arriving, sems, number):
+        return remote(
+            pad.at[f_edge[m] if arriving else frame_of[m], row],
+            pad.at[f_edge[m] if arriving else frames + 1 - f_edge[m], row],
+            sems[0].at[number],
+            sems[1].at[number],
+            (f_target[m], p_me, t_me),
+        )
+
+    def side_copy(part, m, arriving):
+        sems = (frame_send, frame_recv)
+        return frame_copy(part, m, order[part] + 1, arriving, sems, 2 * part + m)
+
+    def corner_copy(part, m, arriving):
+        sems = (corner_send, corner_recv)
+        return frame_copy(part, m, edge[part], arriving, sems, 2 * part + m)
+
+    def when(condition, action):
+        if condition is None:
+            action()
+        else:
+            pl.when(condition)(action)
+
+    row_ok = (None, next_there)
+
+    def corner_ok(part, m):
+        return f_ok[m] if part == 0 else jnp.logical_and(next_there, f_ok[m])
+
+    def send_rows(part):
+        for m in range(2):
+            when(row_ok[part], row_copy(part, m, False).start)
 
     for part in range(2):
-        for d in (-1, 1):
-            pl.when(p_there[d])(row_copy(d, part).start)
-    for d in (-1, 1):
-        pl.when(f_there[d])(frame_copy(d).start)
+        dequantize(part)
+        if part == 0:
+            pl.semaphore_wait(barrier, count)
+            send_rows(0)
+        for m in range(2):
+            when(f_ok[m], side_copy(part, m, False).start)
 
     loads[2].wait()
     own_lanes = pl.ds(pl.multiple_of(t_me * channels, LANES), channels)
@@ -219,38 +242,35 @@
         for b in range(3):
             taps[a * 3 + b] = taps_ref[a, b, :, own_lanes].astype(jnp.float32)
 
-    for part in range(2):
-        for g in (-1, 1):
-            pl.when(p_there[-g])(row_copy(g, part).wait_recv)
-            for d in (-1, 1):
-                first = (lead == 1) if d < 0 else (lead == 0)
-                mine = first if part == 0 else jnp.logical_not(first)
-                ready = jnp.logical_and(jnp.logical_and(p_there[-g], f_there[d]), mine)
-                pl.when(ready)(corner_copy(d, g).start)
-    for d in (-1, 1):
-        pl.when(f_there[-d])(frame_copy(d).wait_recv)
+    for m in range(2):
+        row_copy(0, m, False).wait_send()
+    send_rows(1)
 
     col = lax.broadcasted_iota(jnp.int32, (cols, LANES), 0)
 
-    def mix_copy(part, r, t):
-        i = order[part] * rows + r
+    def mix_copy(part, f, t):
+        i = f * rows + order[part]
         return pltpu.make_async_remote_copy(
             src_ref=mixed.at[i, t],
             dst_ref=mixed.at[i, t],
-            send_sem=mix_send.at[part * rows + r],
-            recv_sem=mix_recv.at[part * rows + r],
+            send_sem=mix_send.at[part * frames + f],
+            recv_sem=mix_recv.at[part * frames + f],
             device_id=(f_me, p_me, t_peer),
             device_id_type=MESH,
         )
 
     for part in range(2):
-        f = order[part]
-        for d in (-1, 1):
-            for g in (-1, 1):
-                needs = (f == 0) if d > 0 else (f == frames - 1)
-                ready = jnp.logical_and(jnp.logical_and(p_there[-g], f_there[-d]), needs)
-                pl.when(ready)(corner_copy(d, g).wait_recv)
-        for r in range(rows):
+        r = order[part]
+        for m in range(2):
+            when(row_ok[part], row_copy(part, m, True).wait_recv)
+            when(corner_ok(part, m), corner_copy(part, m, False).start)
+        if part == 0:
+            for both in range(2):
+                for m in range(2):
+                    when(f_ok[m], side_copy(both, m, True).wait_recv)
+        for m in range(2):
+            when(corner_ok(part, m), corner_copy(part, m, True).wait_recv)
+        for f in range(frames):
 
             def conv(step, carry):
                 at = pl.ds(pl.multiple_of(step * LANES, LANES), LANES)
@@ -271,7 +291,7 @@
                 return carry
 
             lax.fori_loop(0, channels // LANES, conv, 0)
-            mix_copy(part, r, t_me).start()
+            mix_copy(part, f, t_me).start()
 
     started = []
 
@@ -323,15 +343,14 @@
         )
         beside(n, 0)
 
+    loads[3].wait()
+    loads[4].wait()
+    picked = [mod_ref[ts_ref[f]].astype(jnp.float32) for f in range(frames)]
     for part in range(2):
-        f = order[part]
-        if part == 0:
-            loads[3].wait()
-            loads[4].wait()
-        picked = mod_ref[ts_ref[f]].astype(jnp.float32)
-        shift, scale = picked[0:1], 1.0 + picked[1:2]
-        for r in range(rows):
-            mix_copy(part, r, t_peer).wait_recv()
+        r = order[part]
+        for f in range(frames):
+            shift, scale = picked[f][0:1], 1.0 + picked[f][1:2]
+            mix_copy(part, f, t_peer).wait_recv()
             xs = [mixed[f * rows + r, t].astype(jnp.float32) for t in range(n_tp)]
             mean = sum(jnp.sum(x, axis=1, keepdims=True) for x in xs) * (1.0 / width)
             xs = [x - mean for x in xs]
@@ -340,7 +359,7 @@
             for t in range(n_tp):
                 at = slice(t * channels, (t + 1) * channels)
                 y = xs[t] * inv * scale[:, at] + shift[:, at]
-                row = part * half + r * cols
+                row = part * half + f * cols
                 normed[row : row + cols, at] = y.astype(jnp.bfloat16)
         if part == 0:
             loads[5].wait()
@@ -359,12 +378,13 @@
             if piece_part == part:
                 spread_piece(n)
 
-    def relay(n):
-        for slot in [2] + [k + s for k in far for s in (0, 2)]:
+    def relay(n, slots):
+        for slot in slots:
             arrivals[n, slot].wait_recv()
             beside(n, slot)
 
-    relay(0)
+    far_slots = [k + s for k in far for s in (0, 2)]
+    relay(0, [2])
 
     loads[7].wait()
     q = jnp.dot(normed[...], wq[...], preferred_element_type=jnp.float32)
@@ -378,18 +398,28 @@
         q_pack.at[pl.ds((1 - side) * heads, heads)], q_peer, q_send.at[0], q_recv.at[0], p_pair
     )
 
-    for n in range(1, len(pieces)):
-        relay(n)
-
-    q_copy.wait_recv()
-    for slot in range(1, n_patch, 2):
-        arrivals[0, slot].wait_recv()
-    o_copies = []
-    own = []
+    relay(0, far_slots)
     zeros = jnp.zeros((half, HEAD_DIM), jnp.float32)
-    for h in range(heads):
-        for slot in range(1, n_patch, 2):
-            arrivals[h + 1, slot].wait_recv()
+
+    def attend(queries, rows_kv, state):
+        scores = lax.dot_general(
+            queries, rows_kv, (((1,), (1,)), ((), ())), preferred_element_type=jnp.float32
+        )
+        top = jnp.max(scores, axis=1, keepdims=True)
+        if state is not None:
+            top = jnp.maximum(top, state[0])
+        exps = jnp.exp(scores - top)
+        total = jnp.sum(exps, axis=1, keepdims=True)
+        summed = jnp.dot(
+            exps.astype(jnp.bfloat16), rows_kv, preferred_element_type=jnp.float32
+        )
+        if state is not None:
+            rescale = jnp.exp(state[0] - top)
+            total = total + state[1] * rescale
+            summed = summed + state[2] * rescale
+        return top, total, summed
+
+    def queries_of(h):
         packed = q_peer[h].astype(jnp.float32)
         peer = jnp.concatenate(
             [
@@ -398,32 +428,44 @@
             ],
             axis=0,
         ).astype(jnp.bfloat16)
-        queries = jnp.concatenate([peer, q_own[side * heads + h]], axis=0)
-        rows_kv = kv_all[h].reshape(n_patch * tokens, 2 * HEAD_DIM)
-        scores = lax.dot_general(
-            queries, rows_kv, (((1,), (1,)), ((), ())), preferred_element_type=jnp.float32
-        )
-        exps = jnp.exp(scores - jnp.max(scores, axis=1, keepdims=True))
-        totals = jnp.sum(exps, axis=1, keepdims=True)
-        summed = jnp.dot(
-            exps.astype(jnp.bfloat16), rows_kv, preferred_element_type=jnp.float32
-        )
-        result = summed[:, HEAD_DIM:] / totals
+        return jnp.concatenate([peer, q_own[side * heads + h]], axis=0)
+
+    def keys_of(h, part):
+        block = kv_all[h, :, part * half : (part + 1) * half]
+        return block.reshape(n_patch * half, 2 * HEAD_DIM)
+
+    queries = []
+    states = []
+    for h in range(heads):
+        relay(h + 1, [2] + far_slots)
+        if h == 0:
+            q_copy.wait_recv()
+            for slot in range(1, n_patch, 2):
+                arrivals[0, slot].wait_recv()
+        queries.append(queries_of(h))
+        states.append(attend(queries[h], keys_of(h, 0), None))
+
+    o_copies = []
+    own = []
+    for h in range(heads):
+        for slot in range(1, n_patch, 2):
+            arrivals[h + 1, slot].wait_recv()
+        _, total, summed = attend(queries[h], keys_of(h, 1), states[h])
+        result = summed[:, HEAD_DIM:] / total
         o_pack[h] = jnp.concatenate(
             [result[:half], result[half:tokens]], axis=1
         ).astype(jnp.bfloat16)
         o_copies.append(go(o_pack.at[h], o_peer.at[h], o_send.at[h], o_recv.at[h], p_pair))
         own.append(result[tokens:])
 
-    for d in (-1, 1):
-        for part in range(2):
-            pl.when(p_there[d])(row_copy(d, part).wait_send)
-        pl.when(f_there[d])(frame_copy(d).wait_send)
-        for g in (-1, 1):
-            pl.when(jnp.logical_and(p_there[-g], f_there[d]))(corner_copy(d, g).wait_send)
     for part in range(2):
-        for r in range(rows):
-            mix_copy(part, r, t_me).wait_send()
+        for m in range(2):
+            if part == 1:
+                when(row_ok[part], row_copy(part, m, False).wait_send)
+            when(f_ok[m], side_copy(part, m, False).wait_send)
+            when(corner_ok(part, m), corner_copy(part, m, False).wait_send)
+        for f in range(frames):
+            mix_copy(part, f, t_me).wait_send()
     for copy in started:
         copy.wait_send()
 
@@ -436,8 +478,9 @@
     high = jnp.concatenate(others + own, axis=1)
     final = jnp.where(side == 0, low, high).astype(jnp.bfloat16)
     for part in range(2):
-        piece = final[part * half : (part + 1) * half]
-        out_ref[order[part]] = piece.reshape(rows, cols, local_width)
+        for f in range(frames):
+            row = part * half + f * cols
+            out_ref[f, order[part]] = final[row : row + cols]
 
 
 def solution(mesh):
@@ -481,11 +524,11 @@
                 pltpu.VMEM((heads, tokens // 2, LANES), bf),
                 pltpu.VMEM((heads, tokens // 2, LANES), bf),
                 pltpu.VMEM((heads, tokens // 2, LANES), bf),
-                dma((8,)),
+                dma((9,)),
                 dma((4,)),
                 dma((4,)),
-                dma((2,)),
-                dma((2,)),
+                dma((4,)),
+                dma((4,)),
                 dma((4,)),
                 dma((4,)),
                 dma((frames * rows,)),

time: 35.6 us -> 36.8 us (1.034)
  Pallas kernels: 33.9 us -> 35.1 us
    pallas_call x1, Pallas kernels: 33.9 us -> 35.1 us  [local(): pl.pallas_call(functools.partial(kernel, sizes), out_shape=jax.ShapeDtype...]
where the time goes in v2:
time: 36.8 us; the launch traced here: 36.7 us
  Pallas kernels  35.1 us (95%)
  local copies, waits for them, and re-layouts  1.54 us (4%)
    pallas_call x1, Pallas kernels, local(): pl.pallas_call(functools.partial(kernel, sizes), out_shape=jax.ShapeDtype...  35.1 us
    unnamed x1, local copies, waits for them, and re-layouts  1.54 us

profile of v2, /device:TPU:0, one launch (start us, length us, event | category | flops | bytes accessed | tf_op | source)
XLA Modules:
  0.0 36.7 jit_solution(6347899943276172790)
XLA Ops:
  0.0 35.1 %shard_map.82 = bf16[2,2,32,384]{3,2,1,0:T(8,128)(2,1)} custom-call(s32[2]{0:T(128)} %ts_hbm.1, s32[2,2,32,768]{3,2,1,0:T(8,128)} %codes_hbm.1, s32[2,12,2,32]{3,2,1,0:T(2,128)} %bitcast.1, bf16[3,3,3,1536]{3,2,1,0:T(4,128)(2,1)} %taps_hbm.1, bf16[50,2,1536]{2,1,0:T(2,128)(2,1)} %mod_hbm.1, bf16[1536,384]{1,0:T(8,128)(2,1)} %wq_hbm.1, ...), custom_call_target="tpu_custom_call" | custom-call | flops 855638016 | bytes 3538944 | tf_op jit(solution)/shard_map/pallas_call | solution.py:503
  35.1 1.5 %copy.10 = bf16[2,2,32,384]{3,2,1,0:T(8,128)(2,1)} copy(bf16[2,2,32,384]{3,2,1,0:T(8,128)(2,1)} %shard_map.82) | data formatting | bytes 196608

commit v3 on v1

--- a/solution.py
+++ b/solution.py
@@ -87,6 +87,7 @@
     order = (lead, 1 - lead)
     p_pair = flip(p_me, 2)
     p_twin = flip(p_me, 1)
+    p_cross = flip(p_me, 3)
     far = list(range(4, n_patch, 4))
 
     loads = [
@@ -104,7 +105,7 @@
             ]
         )
     ]
-    for copy in loads:
+    for copy in loads[:2]:
         copy.start()
 
     barrier = pltpu.get_barrier_semaphore()
@@ -114,7 +115,7 @@
 
     f_there = {-1: f_me > 0, 1: f_me < n_frame - 1}
     p_there = {-1: p_me > 0, 1: p_me < n_patch - 1}
-    count = 3 + 2 * len(far)
+    count = 4 + 2 * len(far)
     for d in (-1, 1):
 
         @pl.when(f_there[d])
@@ -129,9 +130,12 @@
     signal(f_me, p_me, t_peer)
     signal(f_me, p_pair, t_me)
     signal(f_me, p_twin, t_me)
+    signal(f_me, p_cross, t_me)
     for k in far:
         signal(f_me, flip(p_me, k), t_me)
         signal(f_me, flip(p_me, k + 2), t_me)
+    for copy in loads[2:]:
+        copy.start()
 
     for d in (-1, 1):
         edge_f = 0 if d < 0 else frames + 1
@@ -320,6 +324,13 @@
                 )
         arrivals[n, 2] = go(
             kv_own.at[other, at], kv_all.at[hs, 2, at], a_send.at[n], a_recv.at[n], p_pair
+        )
+        arrivals[n, 3] = go(
+            kv_own.at[other, at],
+            kv_all.at[hs, 3, at],
+            c_send.at[n, 1],
+            c_recv.at[n, 1],
+            p_cross,
         )
         beside(n, 0)
 
@@ -360,11 +371,9 @@
                 spread_piece(n)
 
     def relay(n):
-        for slot in [2] + [k + s for k in far for s in (0, 2)]:
+        for slot in [k + s for k in far for s in (0, 2)]:
             arrivals[n, slot].wait_recv()
             beside(n, slot)
-
-    relay(0)
 
     loads[7].wait()
     q = jnp.dot(normed[...], wq[...], preferred_element_type=jnp.float32)
@@ -378,17 +387,17 @@
         q_pack.at[pl.ds((1 - side) * heads, heads)], q_peer, q_send.at[0], q_recv.at[0], p_pair
     )
 
-    for n in range(1, len(pieces)):
+    for n in range(len(pieces)):
         relay(n)
 
     q_copy.wait_recv()
-    for slot in range(1, n_patch, 2):
+    for slot in [2] + list(range(1, n_patch, 2)):
         arrivals[0, slot].wait_recv()
     o_copies = []
     own = []
     zeros = jnp.zeros((half, HEAD_DIM), jnp.float32)
     for h in range(heads):
-        for slot in range(1, n_patch, 2):
+        for slot in [2] + list(range(1, n_patch, 2)):
             arrivals[h + 1, slot].wait_recv()
         packed = q_peer[h].astype(jnp.float32)
         peer = jnp.concatenate(

time: 35.6 us -> 34.9 us (0.980)
  Pallas kernels: 33.9 us -> 33.2 us
    pallas_call x1, Pallas kernels: 33.9 us -> 33.2 us  [local(): pl.pallas_call(functools.partial(kernel, sizes), out_shape=jax.ShapeDtype...]
where the time goes in v3:
time: 34.9 us; the launch traced here: 34.8 us
  Pallas kernels  33.2 us (95%)
  local copies, waits for them, and re-layouts  1.54 us (4%)
    pallas_call x1, Pallas kernels, local(): pl.pallas_call(functools.partial(kernel, sizes), out_shape=jax.ShapeDtype...  33.2 us
    unnamed x1, local copies, waits for them, and re-layouts  1.54 us

profile of v3, /device:TPU:0, one launch (start us, length us, event | category | flops | bytes accessed | tf_op | source)
XLA Modules:
  0.0 34.8 jit_solution(8725725210104525578)
XLA Ops:
  0.0 33.2 %shard_map.82 = bf16[2,2,32,384]{3,2,1,0:T(8,128)(2,1)} custom-call(s32[2]{0:T(128)} %ts_hbm.1, s32[2,2,32,768]{3,2,1,0:T(8,128)} %codes_hbm.1, s32[2,12,2,32]{3,2,1,0:T(2,128)} %bitcast.1, bf16[3,3,3,1536]{3,2,1,0:T(4,128)(2,1)} %taps_hbm.1, bf16[50,2,1536]{2,1,0:T(2,128)(2,1)} %mod_hbm.1, bf16[1536,384]{1,0:T(8,128)(2,1)} %wq_hbm.1, ...), custom_call_target="tpu_custom_call" | custom-call | flops 855638016 | bytes 3538944 | tf_op jit(solution)/shard_map/pallas_call | solution.py:469
  33.2 1.5 %copy.10 = bf16[2,2,32,384]{3,2,1,0:T(8,128)(2,1)} copy(bf16[2,2,32,384]{3,2,1,0:T(8,128)(2,1)} %shard_map.82) | data formatting | bytes 196608

commit v4 on v3

--- a/solution.py
+++ b/solution.py
@@ -94,7 +94,7 @@
         pltpu.make_async_copy(src, dst, in_sem.at[i])
         for i, (src, dst) in enumerate(
             [
-                (codes_hbm, codes_ref),
+                (codes_hbm.at[order[1]], codes_ref.at[order[1]]),
                 (exps_hbm, exps_ref),
                 (taps_hbm, taps_ref),
                 (ts_hbm, ts_ref),
@@ -102,11 +102,12 @@
                 (wk_hbm, wkv.at[:, pl.ds(0, local_width)]),
                 (wv_hbm, wkv.at[:, pl.ds(local_width, local_width)]),
                 (wq_hbm, wq),
+                (codes_hbm.at[order[0]], codes_ref.at[order[0]]),
             ]
         )
     ]
-    for copy in loads[:2]:
-        copy.start()
+    for i in (0, 1, 8):
+        loads[i].start()
 
     barrier = pltpu.get_barrier_semaphore()
 
@@ -134,7 +135,7 @@
     for k in far:
         signal(f_me, flip(p_me, k), t_me)
         signal(f_me, flip(p_me, k + 2), t_me)
-    for copy in loads[2:]:
+    for copy in loads[2:8]:
         copy.start()
 
     for d in (-1, 1):
@@ -162,9 +163,9 @@
         lax.broadcasted_iota(jnp.int32, (groups, channels), 1) // span
         == lax.broadcasted_iota(jnp.int32, (groups, channels), 0)
     ).astype(jnp.float32).astype(jnp.bfloat16)
-    loads[0].wait()
     loads[1].wait()
-    for f in range(frames):
+
+    def dequantize(f):
         for r in range(rows):
             factor = jnp.left_shift(jnp.ones((groups, cols), jnp.int32), exps_ref[f, :, r, :] + 8)
             factor = (factor.astype(jnp.float32) * (2.0**-8)).astype(jnp.bfloat16)
@@ -173,8 +174,6 @@
             )
             values = codes_ref[f, r].astype(jnp.float32) * factor
             pad[f + 1, r + 1] = values.astype(jnp.bfloat16)
-
-    pl.semaphore_wait(barrier, count)
 
     def row_copy(d, part):
         frame = 1 + order[1 - part]
@@ -212,6 +211,10 @@
         )
 
     for part in range(2):
+        loads[0 if part == 0 else 8].wait()
+        dequantize(order[1 - part])
+        if part == 0:
+            pl.semaphore_wait(barrier, count)
         for d in (-1, 1):
             pl.when(p_there[d])(row_copy(d, part).start)
     for d in (-1, 1):
@@ -396,6 +399,18 @@
     o_copies = []
     own = []
     zeros = jnp.zeros((half, HEAD_DIM), jnp.float32)
+
+    def attend(queries, rows_kv):
+        scores = lax.dot_general(
+            queries, rows_kv, (((1,), (1,)), ((), ())), preferred_element_type=jnp.float32
+        )
+        exps = jnp.exp(scores - jnp.max(scores, axis=1, keepdims=True))
+        totals = jnp.sum(exps, axis=1, keepdims=True)
+        summed = jnp.dot(
+            exps.astype(jnp.bfloat16), rows_kv, preferred_element_type=jnp.float32
+        )
+        return summed[:, HEAD_DIM:] / totals
+
     for h in range(heads):
         for slot in [2] + list(range(1, n_patch, 2)):
             arrivals[h + 1, slot].wait_recv()
@@ -407,22 +422,16 @@
             ],
             axis=0,
         ).astype(jnp.bfloat16)
-        queries = jnp.concatenate([peer, q_own[side * heads + h]], axis=0)
+        mine = q_own[side * heads + h]
         rows_kv = kv_all[h].reshape(n_patch * tokens, 2 * HEAD_DIM)
-        scores = lax.dot_general(
-            queries, rows_kv, (((1,), (1,)), ((), ())), preferred_element_type=jnp.float32
-        )
-        exps = jnp.exp(scores - jnp.max(scores, axis=1, keepdims=True))
-        totals = jnp.sum(exps, axis=1, keepdims=True)
-        summed = jnp.dot(
-            exps.astype(jnp.bfloat16), rows_kv, preferred_element_type=jnp.float32
-        )
-        result = summed[:, HEAD_DIM:] / totals
+        last = h == heads - 1
+        queries = peer if last else jnp.concatenate([peer, mine], axis=0)
+        result = attend(queries, rows_kv)
         o_pack[h] = jnp.concatenate(
             [result[:half], result[half:tokens]], axis=1
         ).astype(jnp.bfloat16)
         o_copies.append(go(o_pack.at[h], o_peer.at[h], o_send.at[h], o_recv.at[h], p_pair))
-        own.append(result[tokens:])
+        own.append(attend(mine, rows_kv) if last else result[tokens:])
 
     for d in (-1, 1):
         for part in range(2):
@@ -490,7 +499,7 @@
                 pltpu.VMEM((heads, tokens // 2, LANES), bf),
                 pltpu.VMEM((heads, tokens // 2, LANES), bf),
                 pltpu.VMEM((heads, tokens // 2, LANES), bf),
-                dma((8,)),
+                dma((9,)),
                 dma((4,)),
                 dma((4,)),
                 dma((2,)),

time: 34.9 us -> 35.1 us (level)
  no operation moved by 1% of the time
where the time goes in v4:
time: 35.1 us; the launch traced here: 34.9 us
  Pallas kernels  33.4 us (95%)
  local copies, waits for them, and re-layouts  1.54 us (4%)
    pallas_call x1, Pallas kernels, local(): pl.pallas_call(functools.partial(kernel, sizes), out_shape=jax.ShapeDtype...  33.4 us
    unnamed x1, local copies, waits for them, and re-layouts  1.54 us

profile of v4, /device:TPU:0, one launch (start us, length us, event | category | flops | bytes accessed | tf_op | source)
XLA Modules:
  0.0 34.9 jit_solution(3975984784763455694)
XLA Ops:
  0.0 33.4 %shard_map.82 = bf16[2,2,32,384]{3,2,1,0:T(8,128)(2,1)} custom-call(s32[2]{0:T(128)} %ts_hbm.1, s32[2,2,32,768]{3,2,1,0:T(8,128)} %codes_hbm.1, s32[2,12,2,32]{3,2,1,0:T(2,128)} %bitcast.1, bf16[3,3,3,1536]{3,2,1,0:T(4,128)(2,1)} %taps_hbm.1, bf16[50,2,1536]{2,1,0:T(2,128)(2,1)} %mod_hbm.1, bf16[1536,384]{1,0:T(8,128)(2,1)} %wq_hbm.1, ...), custom_call_target="tpu_custom_call" | custom-call | flops 855638016 | bytes 3538944 | tf_op jit(solution)/shard_map/pallas_call | solution.py:478
  33.4 1.5 %copy.10 = bf16[2,2,32,384]{3,2,1,0:T(8,128)(2,1)} copy(bf16[2,2,32,384]{3,2,1,0:T(8,128)(2,1)} %shard_map.82) | data formatting | bytes 196608

commit v5 on v4

--- a/solution.py
+++ b/solution.py
@@ -520,7 +520,7 @@
                 dma((heads,)),
             ],
             compiler_params=pltpu.CompilerParams(
-                collective_id=0, has_side_effects=True, vmem_limit_bytes=56 * 1024 * 1024
+                collective_id=0, has_side_effects=True, vmem_limit_bytes=55040 * 1024
             ),
             cost_estimate=pl.CostEstimate(
                 flops=2 * macs, bytes_accessed=width * local_width * 6, transcendentals=0

time: 35.1 us -> 35 us (level)
  Pallas kernels: 33.4 us -> 32.8 us
  local copies, waits for them, and re-layouts: 1.54 us -> 2.03 us
    pallas_call x1, Pallas kernels: 33.4 us -> 32.8 us  [local(): pl.pallas_call(functools.partial(kernel, sizes), out_shape=jax.ShapeDtype...]
    unnamed x1 -> x5, local copies, waits for them, and re-layouts: 1.54 us -> 2.03 us
where the time goes in v5:
time: 35 us; the launch traced here: 34.8 us
  Pallas kernels  32.8 us (94%)
  local copies, waits for them, and re-layouts  2.03 us (6%)
    pallas_call x1, Pallas kernels, local(): pl.pallas_call(functools.partial(kernel, sizes), out_shape=jax.ShapeDtype...  32.8 us
    unnamed x5, local copies, waits for them, and re-layouts  2.03 us

profile of v5, /device:TPU:0, one launch (start us, length us, event | category | flops | bytes accessed | tf_op | source)
XLA Modules:
  0.0 34.8 jit_solution(1879447316797368962)
XLA Ops:
  0.0 0.0 copy-start
  0.0 0.7 %copy-done = s32[2,2,32,12]{2,1,3,0:T(2,128)S(1)} copy-done((s32[2,2,32,12]{2,1,3,0:T(2,128)S(1)}, s32[2,2,32,12]{2,1,3,0:T(2,128)}, u32[]{:S(2)}) %copy-start) | copy-done | bytes 6168
  0.7 0.0 copy-start.1
  0.7 0.7 %copy-done.1 = s32[2]{0:T(128)S(1)} copy-done((s32[2]{0:T(128)S(1)}, s32[2]{0:T(128)}, u32[]{:S(2)}) %copy-start.1) | copy-done | bytes 32
  1.4 32.8 %shard_map.82 = bf16[2,2,32,384]{3,2,1,0:T(8,128)(2,1)S(1)} custom-call(s32[2]{0:T(128)S(1)} %copy-done.1, s32[2,2,32,768]{3,2,1,0:T(8,128)} %codes_hbm.1, s32[2,12,2,32]{3,2,1,0:T(2,128)S(1)} %bitcast.1, bf16[3,3,3,1536]{3,2,1,0:T(4,128)(2,1)} %taps_hbm.1, bf16[50,2,1536]{2,1,0:T(2,128)(2,1)} %mod_hbm.1, bf16[1536,384]{1,0:T(8,128)(2,1)} %wq_hbm.1, ...), custom_call_target="tpu_custom_call" | custom-call | flops 855638016 | bytes 3538944 | tf_op jit(solution)/shard_map/pallas_call | solution.py:478
  34.2 0.6 %copy.10 = bf16[2,2,32,384]{3,2,1,0:T(8,128)(2,1)} copy(bf16[2,2,32,384]{3,2,1,0:T(8,128)(2,1)S(1)} %shard_map.82) | data formatting | bytes 196608
Async XLA Ops:
  0.0 0.7 %copy-start = (s32[2,2,32,12]{2,1,3,0:T(2,128)S(1)}, s32[2,2,32,12]{2,1,3,0:T(2,128)}, u32[]{:S(2)}) copy-start(s32[2,2,32,12]{2,1,3,0:T(2,128)} %param.9) | copy-start | bytes 18436
  0.7 0.7 %copy-start.1 = (s32[2]{0:T(128)S(1)}, s32[2]{0:T(128)}, u32[]{:S(2)}) copy-start(s32[2]{0:T(128)} %ts_hbm.1) | copy-start | bytes 28
